TPU v7x, 128 devices: a whole 4x4x4 slice. The times are simulated.
128 devices in a mesh: section: 8 (over y, core), ed: 16 (over x, z).
Axes of the slice: x: 4, y: 4, z: 4, core: 2. Of those that a mesh axis runs over, the one named last changes fastest.
Arguments:
- x_in: bfloat16 [8, 2048, 4096], P('section', 'ed')
- ids_a: int32 [8, 2048, 2], P('section', 'ed'), may hold values from 0 to 15, as said below
- gates_a: float32 [8, 2048, 2], P('section', 'ed'), may hold values from 0.1 to 1
- x_saved: bfloat16 [8, 2048, 4096], P('section', 'ed')
- ids_b: int32 [8, 2048, 2], P('section', 'ed'), may hold values from 0 to 15, as said below
- gates_b: float32 [8, 2048, 2], P('section', 'ed'), may hold values from 0.1 to 1
- dy_in: bfloat16 [8, 2048, 4096], P('section', 'ed'), may hold values from -6 to 6
- gain: float32 [8, 4096], P('section'), may hold values from 0.1 to 1.9
- w_gate: bfloat16 [8, 4096, 12288], P('section', None, 'ed'), may hold values from -0.09375 to 0.09375
- w_up: bfloat16 [8, 4096, 12288], P('section', None, 'ed'), may hold values from -0.09375 to 0.09375
- w_down: bfloat16 [8, 12288, 4096], P('section', 'ed'), may hold values from -0.0546875 to 0.0546875
Outputs:
- mixed: bfloat16 [8, 2048, 4096], P('section', 'ed')
- input_grad: bfloat16 [8, 2048, 4096], P('section', 'ed')
Inputs may be any that keep to these rules, and one draw needn't show every extreme that they name: `ids_a`: each token names two different experts; among the tokens of one ed index and one section at most 32 name expert 0, at least one name it, and in every section some ed index has exactly 32. `ids_b`: each token names two different experts; among the tokens of one ed index and one section at most 32 name expert 0, at least one name it, and in every section some ed index has exactly 32.
All inputs are finite; a program needn't handle non-finite values.
Results may differ from a plain program's by a relative error of at most 0.0039.
Values may be sent and summed in bfloat16 or wider, within the bound.
A program may use at most 128 MiB of HBM per device.

v0:
```python
import jax
import jax.numpy as jnp
from jax import lax
from jax.sharding import PartitionSpec as P

EPSILON = 1e-06


def from_behind(value, axis, steps):
    count = lax.axis_size(axis)
    pairs = [(source, (source + steps) % count) for source in range(count)]
    return lax.ppermute(value, axis, pairs)


def normalize(inputs, gain_row):
    values = inputs.astype(jnp.float32)
    scale = lax.rsqrt(jnp.mean(values * values, axis=-1, keepdims=True) + EPSILON)
    return (values, scale, (values * scale * gain_row).astype(jnp.bfloat16))


def routing(expert_ids, gate_values, capacity):
    chosen = expert_ids == 0
    routed_flag = jnp.any(chosen, axis=1)
    share = jnp.sum(jnp.where(chosen, gate_values, 0.0), axis=1)
    position = jnp.cumsum(routed_flag.astype(jnp.int32)) - 1
    token_slot = jnp.where(routed_flag, position, capacity)
    token_count = expert_ids.shape[0]
    matches = (token_slot[None, :] == jnp.arange(capacity, dtype=jnp.int32)[:, None]).astype(
        jnp.int32
    )
    filled = jnp.sum(matches, axis=1)
    slot_token = (
        jnp.sum(matches * jnp.arange(token_count, dtype=jnp.int32)[None, :], axis=1)
        + (1 - filled) * token_count
    )
    return (token_slot, slot_token, share)


def padded(row_block):
    return jnp.concatenate([row_block, jnp.zeros((1, row_block.shape[1]), row_block.dtype)], axis=0)


def shards(x_in, ids_a, gates_a, x_saved, ids_b, gates_b, dy_in, gain, w_gate, w_up, w_down):
    moving = from_behind(x_in, "section", 1)[0]
    cotangent = from_behind(dy_in, "section", -1)[0]
    tokens_here = moving.shape[0]
    capacity = tokens_here // 4
    gain_row = gain[0]
    gate_slice = w_gate[0]
    up_slice = w_up[0]
    down_slice = w_down[0]
    contract = (((1,), (1,)), ((), ()))
    _, _, normed_a = normalize(moving, gain_row)
    slot_of_a, token_of_a, share_a = routing(ids_a[0], gates_a[0], capacity)
    send_fwd = padded(normed_a)[token_of_a]
    values_b, scale_b, normed_b = normalize(x_saved[0], gain_row)
    slot_of_b, token_of_b, share_b = routing(ids_b[0], gates_b[0], capacity)
    pair_cot = (share_b[:, None] * cotangent.astype(jnp.float32)).astype(jnp.bfloat16)
    send_bwd = padded(normed_b)[token_of_b]
    send_cot = padded(pair_cot)[token_of_b]
    row_block = lax.all_gather(send_fwd, "ed", axis=0, tiled=True)
    gate_pre = jnp.dot(row_block, gate_slice, preferred_element_type=jnp.float32)
    up_pre = jnp.dot(row_block, up_slice, preferred_element_type=jnp.float32)
    hidden = (jax.nn.silu(gate_pre) * up_pre).astype(jnp.bfloat16)
    fwd_terms = jnp.dot(hidden, down_slice, preferred_element_type=jnp.float32)
    fwd_sums = lax.psum_scatter(
        fwd_terms.astype(jnp.bfloat16), "ed", scatter_dimension=0, tiled=True
    )
    stacked = jnp.stack((send_bwd, send_cot), axis=1)
    segment = lax.all_gather(stacked, "ed", axis=0, tiled=True)
    row_block = segment[:, 0]
    gate_pre = jnp.dot(row_block, gate_slice, preferred_element_type=jnp.float32)
    up_pre = jnp.dot(row_block, up_slice, preferred_element_type=jnp.float32)
    sigmoid_gate = jax.nn.sigmoid(gate_pre)
    hidden_grad = lax.dot_general(
        segment[:, 1], down_slice, contract, preferred_element_type=jnp.float32
    )
    gate_grad = (
        hidden_grad * up_pre * (sigmoid_gate * (1.0 + gate_pre * (1.0 - sigmoid_gate)))
    ).astype(jnp.bfloat16)
    up_grad = (hidden_grad * (gate_pre * sigmoid_gate)).astype(jnp.bfloat16)
    back = lax.dot_general(gate_grad, gate_slice, contract, preferred_element_type=jnp.float32)
    bwd_terms = back + lax.dot_general(
        up_grad, up_slice, contract, preferred_element_type=jnp.float32
    )
    bwd_sums = lax.psum_scatter(bwd_terms, "ed", scatter_dimension=0, tiled=True)
    expert_out = padded(fwd_sums)[slot_of_a].astype(jnp.float32)
    mixed = moving.astype(jnp.float32) + share_a[:, None] * expert_out
    pair_back = padded(bwd_sums.astype(jnp.bfloat16))[slot_of_b].astype(jnp.float32)
    weighted = pair_back * gain_row
    average = jnp.mean(weighted * values_b, axis=-1, keepdims=True)
    input_grad = cotangent.astype(jnp.float32) + scale_b * (
        weighted - values_b * scale_b * scale_b * average
    )
    return (mixed.astype(jnp.bfloat16)[None], input_grad.astype(jnp.bfloat16)[None])


def solution(mesh):
    return jax.shard_map(
        shards,
        mesh=mesh,
        in_specs=(
            P("section", "ed", None),
            P("section", "ed", None),
            P("section", "ed", None),
            P("section", "ed", None),
            P("section", "ed", None),
            P("section", "ed", None),
            P("section", "ed", None),
            P("section", None),
            P("section", None, "ed"),
            P("section", None, "ed"),
            P("section", "ed", None),
        ),
        out_specs=(P("section", "ed", None), P("section", "ed", None)),
        check_vma=False,
    )
```

profile of v0, /device:TPU:0, one launch (start us, length us, event | category | flops | bytes accessed | tf_op | source)
XLA Modules:
  0.0 389.7 jit_solution(12688665773752564821)
XLA Ops:
  7.2 2.5 collective-permute-start.1
  9.8 0.7 fusion.55
  10.5 1.5 fusion.34
  12.0 1.6 fusion.36
  14.4 0.7 gather_fusion.2
  15.1 7.3 %collective-permute-done.1 = bf16[1,128,4096]{2,1,0:T(8,128)(2,1)S(1)} collective-permute-done((bf16[1,128,4096]{2,1,0:T(8,128)(2,1)}, bf16[1,128,4096]{2,1,0:T(8,128)(2,1)S(1)}, u32[]{:S(2)}, u32[]{:S(2)}) %collective-permute-start.1) | collective-permute-done | bytes 1048608 | tf_op jit(solution)/shard_map/ppermute | solution.py:12
  22.8 0.6 copy-done.1
  23.4 0.7 gather_fusion.3
  24.1 0.8 pad_maximum_fusion
  25.0 73.2 %all-gather.4.cloned.1.call-done = bf16[512,2,4096]{2,0,1:T(8,128)(2,1)} async-done(((bf16[32,2,4096]{2,0,1:T(8,128)(2,1)}), bf16[512,2,4096]{2,0,1:T(8,128)(2,1)}) %all-gather.4.cloned.1.call-update) | async-done | bytes 8388624 | tf_op jit(solution)/shard_map/all_gather | solution.py:70
  98.2 8.9 %fusion = f32[512,768]{1,0:T(8,128)} fusion(bf16[1,768,4096]{2,1,0:T(8,128)(2,1)} %param.21, bf16[512,2,4096]{2,0,1:T(8,128)(2,1)} %all-gather.4.cloned.1.call-done), kind=kOutput, calls=%fused_computation.5 | convolution fusion | flops 3221225472 | bytes 12058624 | tf_op jit(solution)/shard_map/dot_general | solution.py:75
  107.1 6.8 %fusion.12 = f32[512,768]{1,0:T(8,128)} fusion(bf16[1,4096,768]{2,1,0:T(8,128)(2,1)} %param.19, bf16[512,2,4096]{2,0,1:T(8,128)(2,1)S(1)} %copy-done.7), kind=kOutput, calls=%fused_computation.17 | convolution fusion | flops 3221225472 | bytes 12058624 | tf_op jit(solution)/shard_map/dot_general | solution.py:72
  113.9 5.6 %fusion.4 = f32[512,4096]{1,0:T(8,128)S(1)} fusion(bf16[1,4096,768]{2,1,0:T(8,128)(2,1)S(1)} %bitcast.109, f32[512,768]{1,0:T(8,128)} %fusion, f32[512,768]{1,0:T(8,128)} %fusion.12), kind=kOutput, calls=%fused_computation.9 | convolution fusion | flops 3223584768 | bytes 17825792 | tf_op jit(solution)/shard_map/dot_general | solution.py:83
  119.5 7.8 %multiply_convert_fusion.1 = bf16[512,768]{1,0:T(8,128)(2,1)S(1)} fusion(f32[512,768]{1,0:T(8,128)S(1)} %copy-done.10, f32[512,768]{1,0:T(8,128)S(1)} %copy-done.9, bf16[1,4096,768]{2,1,0:T(8,128)(2,1)} %param.20, bf16[512,2,4096]{2,0,1:T(8,128)(2,1)} %all-gather.4.cloned.1.call-done), kind=kOutput, calls=%fused_computation.56 | convolution fusion | flops 3225157632 | bytes 14417920 | tf_op jit(solution)/shard_map/dot_general | solution.py:73
  127.3 5.7 %fusion.16 = f32[512,4096]{1,0:T(8,128)} fusion(f32[512,4096]{1,0:T(8,128)S(1)} %fusion.4, bf16[512,768]{1,0:T(8,128)(2,1)S(1)} %multiply_convert_fusion.1, bf16[1,4096,768]{2,1,0:T(8,128)(2,1)S(1)} %bitcast.100), kind=kOutput, calls=%fused_computation.21 | convolution fusion | flops 3223322624 | bytes 23855104 | tf_op jit(solution)/shard_map/dot_general | solution.py:82
  133.3 1.0 copy-done.8
  135.0 14.7 %collective-permute-done = bf16[1,128,4096]{2,1,0:T(8,128)(2,1)S(1)} collective-permute-done((bf16[1,128,4096]{2,1,0:T(8,128)(2,1)S(1)}, bf16[1,128,4096]{2,1,0:T(8,128)(2,1)S(1)}, u32[]{:S(2)}, u32[]{:S(2)}) %collective-permute-start) | collective-permute-done | bytes 1048608 | tf_op jit(solution)/shard_map/ppermute | solution.py:12
  150.0 68.0 %reduce-scatter.5.cloned.1.call-done = f32[32,4096]{1,0:T(8,128)} async-done(((f32[512,4096]{1,0:T(8,128)}), f32[32,4096]{1,0:T(8,128)}) %reduce-scatter.5.cloned.1.call-update) | async-done | bytes 524304 | tf_op jit(solution)/shard_map/reduce_scatter | solution.py:86
  218.0 1.1 convert_element_type.137
  219.1 1.2 gather_fusion.4
  220.3 0.6 fusion.37
  221.0 1.1 concatenate.15
  222.1 3.0 gather_fusion
  225.2 51.0 %all-gather.6.cloned.1.call-done = bf16[512,4096]{1,0:T(8,128)(2,1)} async-done(((bf16[32,4096]{1,0:T(8,128)(2,1)}), bf16[512,4096]{1,0:T(8,128)(2,1)}) %all-gather.6.cloned.1.call-update) | async-done | bytes 4194320 | tf_op jit(solution)/shard_map/all_gather | solution.py:61
  276.3 8.7 %fusion.14 = f32[512,768]{1,0:T(8,128)} fusion(bf16[512,4096]{1,0:T(8,128)(2,1)} %all-gather.6.cloned.1.call-done, bf16[1,4096,768]{2,1,0:T(8,128)(2,1)} %param.19), kind=kOutput, calls=%fused_computation.19 | convolution fusion | flops 3221225472 | bytes 12058624 | tf_op jit(solution)/shard_map/dot_general | solution.py:62
  285.0 17.0 %fusion.19 = bf16[512,4096]{1,0:T(8,128)(2,1)} fusion(bf16[1,768,4096]{2,1,0:T(8,128)(2,1)} %param.21, f32[512,768]{1,0:T(8,128)} %fusion.14, bf16[512,4096]{1,0:T(8,128)(2,1)} %all-gather.6.cloned.1.call-done, bf16[1,4096,768]{2,1,0:T(8,128)(2,1)} %param.20), kind=kOutput, calls=%fused_computation.22 | convolution fusion | flops 6446907392 | bytes 22544384 | tf_op jit(solution)/shard_map/dot_general | solution.py:65
  302.0 0.6 copy-done.6
  302.6 3.0 fusion.31
  305.6 73.9 %reduce-scatter.3.cloned.1.call-done = bf16[32,4096]{1,0:T(8,128)(2,1)} async-done(((bf16[512,4096]{1,0:T(8,128)(2,1)}), bf16[32,4096]{1,0:T(8,128)(2,1)}) %reduce-scatter.3.cloned.1.call-update) | async-done | bytes 262160 | tf_op jit(solution)/shard_map/reduce_scatter | solution.py:66
  379.6 1.0 concatenate.16
  380.5 1.2 gather_fusion.1
  381.7 1.4 fusion.30
  (69 shorter events, 2.7 us)
Async XLA Ops:
  7.2 91.0 %all-gather.4.cloned.1.call-start = ((), (), s32[]{:S(2)}) async-start(), calls=%async_computation.3 | async-start | bytes 8912896 | tf_op jit(solution)/shard_map/all_gather | solution.py:70
  7.2 15.2 %collective-permute-start.1 = (bf16[1,128,4096]{2,1,0:T(8,128)(2,1)}, bf16[1,128,4096]{2,1,0:T(8,128)(2,1)S(1)}, u32[]{:S(2)}, u32[]{:S(2)}) collective-permute-start(bf16[1,128,4096]{2,1,0:T(8,128)(2,1)} %param.17), channel_id=1, source_target_pairs={{0,112},{16,0},{32,16},{48,32},{64,48},{80,64},{96,80},{112,96},{1... | collective-permute-start | bytes 3145736 | tf_op jit(solution)/shard_map/ppermute | solution.py:12
  14.0 1.1 copy-start.3
  14.0 1.1 copy-start.4
  22.4 1.0 copy-start.1
  24.9 193.1 %reduce-scatter.5.cloned.1.call-start = ((), (), s32[]{:S(2)}) async-start(), calls=%async_computation.4 | async-start | bytes 8912896 | tf_op jit(solution)/shard_map/reduce_scatter | solution.py:86
  98.2 8.9 %copy-start.7 = (bf16[512,2,4096]{2,0,1:T(8,128)(2,1)S(1)}, bf16[512,2,4096]{2,0,1:T(8,128)(2,1)}, u32[]{:S(2)}) copy-start(bf16[512,2,4096]{2,0,1:T(8,128)(2,1)} %all-gather.4.cloned.1.call-done) | copy-start | bytes 25165828
  98.2 15.7 %slice-start.2 = ((s8[6291456]{0:T(1024)(128)(4,1)}), s8[4194304]{0:T(1024)(128)(4,1)S(1)}, s32[]{:S(2)}) async-start(s8[6291456]{0:T(1024)(128)(4,1)} %bitcast.108), calls=%async_computation.8 | async-start | bytes 8388608
  107.1 6.8 %slice-start.3 = ((s8[6291456]{0:T(1024)(128)(4,1)}), s8[2097152]{0:T(1024)(128)(4,1)S(1)}, s32[]{:S(2)}) async-start(s8[6291456]{0:T(1024)(128)(4,1)} %bitcast.108), calls=%async_computation.9 | async-start | bytes 4194304
  113.9 5.6 %copy-start.9 = (f32[512,768]{1,0:T(8,128)S(1)}, f32[512,768]{1,0:T(8,128)}, u32[]{:S(2)}) copy-start(f32[512,768]{1,0:T(8,128)} %fusion) | copy-start | bytes 4718596
  113.9 5.6 %copy-start.10 = (f32[512,768]{1,0:T(8,128)S(1)}, f32[512,768]{1,0:T(8,128)}, u32[]{:S(2)}) copy-start(f32[512,768]{1,0:T(8,128)} %fusion.12) | copy-start | bytes 4718596
  113.9 13.4 %slice-start = ((s8[6291456]{0:T(1024)(128)(4,1)}), s8[4194304]{0:T(1024)(128)(4,1)S(1)}, s32[]{:S(2)}) async-start(s8[6291456]{0:T(1024)(128)(4,1)} %bitcast.99), calls=%async_computation.6 | async-start | bytes 8388608
  119.5 7.8 %slice-start.1 = ((s8[6291456]{0:T(1024)(128)(4,1)}), s8[2097152]{0:T(1024)(128)(4,1)S(1)}, s32[]{:S(2)}) async-start(s8[6291456]{0:T(1024)(128)(4,1)} %bitcast.99), calls=%async_computation.7 | async-start | bytes 4194304
  133.1 1.2 copy-start.8
  133.1 1.2 copy-start.5
  133.1 143.1 %all-gather.6.cloned.1.call-start = ((), (), s32[]{:S(2)}) async-start(), calls=%async_computation.5 | async-start | bytes 4456448 | tf_op jit(solution)/shard_map/all_gather | solution.py:61
  134.3 15.4 %collective-permute-start = (bf16[1,128,4096]{2,1,0:T(8,128)(2,1)S(1)}, bf16[1,128,4096]{2,1,0:T(8,128)(2,1)S(1)}, u32[]{:S(2)}, u32[]{:S(2)}) collective-permute-start(bf16[1,128,4096]{2,1,0:T(8,128)(2,1)S(1)} %copy-done.8), channel_id=1, source_target_pairs={{0,16},{16,32},{32,48},{48,64},{64,80},{80,96},{96,112},{112,0},{1... | collective-permute-start | bytes 3145736 | tf_op jit(solution)/shard_map/ppermute | solution.py:12
  219.1 1.2 copy-start
  219.1 1.2 copy-start.2
  225.2 154.4 %reduce-scatter.3.cloned.1.call-start = ((), (), s32[]{:S(2)}) async-start(), calls=%async_computation.2 | async-start | bytes 4456448 | tf_op jit(solution)/shard_map/reduce_scatter | solution.py:66
  301.9 0.7 copy-start.6
Sparse Core Ops, SparseCore 0:
  25.1 73.0 all-gather.3
  133.2 84.7 reduce-scatter.4
  225.3 50.9 all-gather.5
  302.1 77.4 reduce-scatter.2
where the time goes:
time: 390 us
  waiting for transfers between devices  288 us (74%)
  matrix products  60.4 us (15%)
  between operations  14 us (4%)
  other arithmetic  12.1 us (3%)
  local copies, waits for them, and re-layouts  11.9 us (3%)
    reduce_scatter x1, waiting for transfers between devices, shards(): lax.psum_scatter(fwd_terms.astype(jnp.bfloat16), 'ed', scatter_dimension=...  73.9 us
    all_gather x1, waiting for transfers between devices, shards(): segment = lax.all_gather(stacked, 'ed', axis=0, tiled=True)  73.2 us
    reduce_scatter x1, waiting for transfers between devices, shards(): lax.psum_scatter(bwd_terms, 'ed', scatter_dimension=0, tiled=True)  68 us
    all_gather x1, waiting for transfers between devices, shards(): row_block = lax.all_gather(send_fwd, 'ed', axis=0, tiled=True)  51 us
    ppermute x2, waiting for transfers between devices, from_behind(): return lax.ppermute(value, axis, pairs)  22 us
    dot_general x1, matrix products, shards(): fwd_terms = jnp.dot(hidden, down_slice, preferred_element_type=jnp.float32)  17 us
    dot_general x2, matrix products, shards(): jnp.dot(row_block, gate_slice, preferred_element_type=jnp.float32)  15.5 us
    dot_general x1, matrix products, shards(): lax.dot_general(segment[:, 1], down_slice, contract, preferred_element_ty...  8.88 us
  transfers between devices with their start and end apart: 6, of which 6 were waited for; matrix products, arithmetic and copies ran while one was open for 2% of the time, Pallas kernels for 0%

commit v1 on v0

v1 whole, which is shorter than its diff:
```python
import functools

import jax
import jax.numpy as jnp
from jax import lax
from jax.experimental import pallas as pl
from jax.experimental.pallas import tpu as pltpu
from jax.sharding import PartitionSpec as P

EPSILON = 1e-06
MESH = pl.DeviceIdType.MESH
SIDE = 4
CAP = 32
PLUS, MINUS = 0, 1
F32, BF16 = jnp.float32, jnp.bfloat16
NT = (((1,), (1,)), ((), ()))


def dot(a, b):
    return jnp.dot(a, b, preferred_element_type=F32)


def dot_nt(a, b):
    return lax.dot_general(a, b, NT, preferred_element_type=F32)


def group(table, half, first, second):
    low, high = first
    if half == 0:
        return table.at[0, low:high, second * CAP : (second + 1) * CAP]
    return table.at[1, second, low * CAP : high * CAP]


def rows_of(table, half, first, rows):
    low, high = rows
    if half == 0:
        return table.at[0, first, low:high]
    return table.at[1, 0, first * CAP + low : first * CAP + high]


def kernel(
    sections,
    route_ref, gain_ref, x_in, x_saved, dy_in, w_gate, w_up, w_down,
    mixed_out, grad_out,
    gate_w, up_w, down_w, tab_b, tab_c, tab_a,
    gate_b, up_b, gate_g, up_g, hidden,
    x_here, saved, cot,
    acc_s0, acc_s1, fin_s0, fin_s1, acc_f, fin_f,
    place_a, place_b, cols, rows_out,
    send_sem, recv_sem, local_sem,
):
    section, ed = lax.axis_index("section"), lax.axis_index("ed")
    x, z = ed // SIDE, ed % SIDE

    def at_x(step):
        return (section, (x + step + SIDE) % SIDE * SIDE + z)

    def at_z(step):
        return (section, x * SIDE + (z + step + SIDE) % SIDE)

    def at_section(step):
        return ((section + step + sections) % sections, ed)

    counter = [0]

    def remote(src, dst, device):
        k = counter[0]
        counter[0] += 1
        return pltpu.make_async_remote_copy(
            src_ref=src, dst_ref=dst, send_sem=send_sem.at[k], recv_sem=recv_sem.at[k],
            device_id=device, device_id_type=MESH,
        )

    def along(half, which, direction):
        step = 1 if direction == PLUS else -1
        on_x = (which == "f") == (half == 0)
        return at_x(step) if on_x else at_z(step)

    width = gate_w.shape[1]
    depth = gate_w.shape[0]
    part = depth // 2
    rows = SIDE * SIDE * CAP
    tokens = saved.shape[0]
    tile = min(256, width)
    half_rows = CAP // 2
    low_rows, high_rows = (0, half_rows), (half_rows, CAP)

    def gather_copies(table):
        made = {}
        for h in (0, 1):
            for d in (PLUS, MINUS):
                back = 3 if d == PLUS else 1
                rows_here = low_rows if d == PLUS else high_rows
                pair = (0, 2) if d == PLUS else (2, 4)
                f, s = along(h, "f", d), along(h, "s", d)
                made[h, d, "near"] = remote(group(table, h, (0, 1), 0), group(table, h, (back, back + 1), 0), f)
                made[h, d, "own"] = remote(group(table, h, (0, 1), 0), group(table, h, (0, 1), back), s)
                made[h, d, "far"] = remote(rows_of(table, h, back, rows_here), rows_of(table, h, 2, rows_here), f)
                made[h, d, "rest"] = remote(group(table, h, (1, 4), 0), group(table, h, (1, 4), back), s)
                made[h, d, "last"] = remote(group(table, h, pair, back), group(table, h, pair, 2), s)
        return made

    def fin_slice(t, half, direction, pair):
        low, high = pair
        if half == 0:
            return fin_s0.at[t, direction, low:high]
        return fin_s1.at[t, direction, low * CAP : high * CAP]

    def scatter_copies(table, t):
        made = {}
        for h in (0, 1):
            acc = acc_s0 if h == 0 else acc_s1
            for d in (PLUS, MINUS):
                near = 1 if d == PLUS else 3
                mine, other = ((0, 2), (2, 4)) if d == PLUS else ((2, 4), (0, 2))
                my_rows, other_rows = (low_rows, high_rows) if d == PLUS else (high_rows, low_rows)
                f, s = along(h, "f", d), along(h, "s", d)
                made[h, d, "sa"] = remote(group(table, h, mine, 2), acc.at[t, d], s)
                made[h, d, "sd"] = remote(group(table, h, other, near), fin_slice(t, h, d, other), s)
                made[h, d, "sf"] = remote(group(table, h, mine, near), fin_slice(t, h, d, mine), s)
                made[h, d, "fa"] = remote(rows_of(table, h, 2, my_rows), acc_f.at[t, h, d], f)
                made[h, d, "fd"] = remote(
                    rows_of(table, h, near, other_rows), fin_f.at[t, h, d, other_rows[0] : other_rows[1]], f
                )
                made[h, d, "ff"] = remote(
                    rows_of(table, h, near, my_rows), fin_f.at[t, h, d, my_rows[0] : my_rows[1]], f
                )
        return made

    both = [(h, d) for h in (0, 1) for d in (PLUS, MINUS)]
    copy_x = remote(x_in.at[0], x_here, at_section(1))
    copy_dy = remote(dy_in.at[0], cot, at_section(-1))
    gather_b, gather_c, gather_a = gather_copies(tab_b), gather_copies(tab_c), gather_copies(tab_a)
    scatter_b, scatter_a = scatter_copies(tab_b, 0), scatter_copies(tab_c, 1)

    def start(copies, *names):
        for name in names:
            for h, d in both:
                copies[h, d, name].start()

    def after(copies, arrived, names):
        for h, d in both:
            for name in arrived:
                copies[h, d, name].wait_recv()
            for name in names:
                copies[h, d, name].start()

    def received(copies, *names):
        for h, d in both:
            for name in names:
                copies[h, d, name].wait_recv()

    def sent(copies):
        for copy in copies.values():
            copy.wait_send()

    def far(copies):
        after(copies, ("near",), ("far",))

    def rest(copies):
        for h in (0, 1):
            for d in (PLUS, MINUS):
                copies[h, d, "far"].wait_recv()
            for d in (PLUS, MINUS):
                copies[h, d, "rest"].start()

    def last(copies):
        after(copies, ("own", "rest"), ("last",))

    def scatter_0(copies, h):
        for name in ("sa", "sd"):
            for d in (PLUS, MINUS):
                copies[h, d, name].start()

    def add_into(target, other):
        target[...] = (target[...].astype(F32) + other[...].astype(F32)).astype(BF16)

    def scatter_1(copies, table, t):
        for h, d in both:
            near = 1 if d == PLUS else 3
            mine = (0, 2) if d == PLUS else (2, 4)
            acc = acc_s0 if h == 0 else acc_s1
            copies[h, d, "sa"].wait_recv()
            add_into(group(table, h, mine, near), acc.at[t, d])
            copies[h, d, "sf"].start()

    def scatter_2(copies, table, t):
        for h in (0, 1):
            for d in (PLUS, MINUS):
                copies[h, d, "sd"].wait_recv()
                copies[h, d, "sf"].wait_recv()
            fin = fin_s0 if h == 0 else fin_s1
            total = group(table, h, (0, 4), 0)
            total[...] = (
                total[...].astype(F32) + fin[t, PLUS].astype(F32) + fin[t, MINUS].astype(F32)
            ).astype(BF16)
            for name in ("fa", "fd"):
                for d in (PLUS, MINUS):
                    copies[h, d, name].start()

    def scatter_3(copies, table, t):
        for h, d in both:
            near = 1 if d == PLUS else 3
            my_rows = low_rows if d == PLUS else high_rows
            copies[h, d, "fa"].wait_recv()
            add_into(rows_of(table, h, near, my_rows), acc_f.at[t, h, d])
            copies[h, d, "ff"].start()

    def scatter_4(copies, table, t):
        for h in (0, 1):
            for d in (PLUS, MINUS):
                copies[h, d, "fd"].wait_recv()
                copies[h, d, "ff"].wait_recv()
            total = (
                rows_of(table, h, 0, (0, CAP))[...].astype(F32)
                + fin_f[t, h, PLUS].astype(F32)
                + fin_f[t, h, MINUS].astype(F32)
            )
            rows_out[t, :, h * part : (h + 1) * part] = total.astype(BF16)

    load_saved = pltpu.make_async_copy(x_saved.at[0], saved, local_sem.at[0])
    load_saved.start()
    loads = [
        pltpu.make_async_copy(src.at[0], dst, local_sem.at[k])
        for k, (src, dst) in enumerate(((w_gate, gate_w), (w_up, up_w), (w_down, down_w)), start=1)
    ]
    barrier = pltpu.get_barrier_semaphore()
    for device in (at_x(1), at_x(-1), at_z(1), at_z(-1), at_section(1), at_section(-1)):
        pl.semaphore_signal(barrier, inc=1, device_id=device, device_id_type=MESH)

    route = route_ref[...]
    upper = (
        lax.broadcasted_iota(jnp.int32, (tokens, tokens), 0) <= lax.broadcasted_iota(jnp.int32, (tokens, tokens), 1)
    )
    diagonal = (
        lax.broadcasted_iota(jnp.int32, (tokens, tokens), 0) == lax.broadcasted_iota(jnp.int32, (tokens, tokens), 1)
    )
    count = dot(route.astype(BF16), upper.astype(BF16))
    slot_rows = lax.broadcasted_iota(jnp.int32, (CAP, tokens), 0).astype(F32)
    slot_cols = lax.broadcasted_iota(jnp.int32, (tokens, CAP), 1).astype(F32)

    def column(row):
        return jnp.sum(jnp.where(diagonal, row, 0.0), axis=1, keepdims=True)

    takes = []
    for t, place in ((0, place_a), (2, place_b)):
        code = jnp.where(route[t : t + 1] > 0.5, count[t : t + 1] - 1.0, -1.0)
        takes.append(jnp.where(code == slot_rows, 1.0, 0.0))
        place[...] = jnp.where(column(code) == slot_cols, 1.0, 0.0).astype(BF16)
    take_a, take_b = takes
    share_slot = jnp.sum(take_b * route[3:4], axis=1, keepdims=True)
    cols[...] = column(route[1:2])
    take_a, take_b = take_a.astype(BF16), take_b.astype(BF16)

    pl.semaphore_wait(barrier, 6)
    copy_x.start()
    copy_dy.start()

    def put_own(table, values):
        for h in (0, 1):
            table[h, 0, 0:CAP, :] = values[:, h * part : (h + 1) * part]

    def normed(values):
        scale = lax.rsqrt(jnp.mean(values * values, axis=-1, keepdims=True) + EPSILON)
        return (values * scale * gain_ref[...]).astype(BF16)

    load_saved.wait()
    put_own(tab_b, normed(dot(take_b, saved[...])))
    start(gather_b, "near", "own")
    for load in loads:
        load.start()
    far(gather_b)
    rest(gather_b)
    copy_dy.wait_recv()
    put_own(tab_c, (share_slot * dot(take_b, cot[...])).astype(BF16))
    start(gather_c, "near", "own")
    copy_x.wait_recv()
    put_own(tab_a, normed(dot(take_a, x_here[...])))
    last(gather_b)
    far(gather_c)
    start(gather_a, "near", "own")
    for load in loads:
        load.wait()
    received(gather_b, "last")

    def tall(table, h):
        return table[h].reshape(rows, part)

    def columns(i):
        return pl.ds(pl.multiple_of(i * tile, tile), tile)

    def project(table, weight, i):
        return dot(tall(table, 0), weight[0:part, columns(i)]) + dot(tall(table, 1), weight[part:depth, columns(i)])

    steps = width // tile

    @pl.loop(0, steps)
    def _(i):
        gate_b[:, columns(i)] = project(tab_b, gate_w, i)
        up_b[:, columns(i)] = project(tab_b, up_w, i)

        @pl.when(i == 0)
        def _():
            rest(gather_c)

    far(gather_a)
    last(gather_c)
    rest(gather_a)
    received(gather_c, "last")

    @pl.loop(0, steps)
    def _(i):
        at = columns(i)
        hidden_grad = dot_nt(tall(tab_c, 0), down_w[at, 0:part]) + dot_nt(tall(tab_c, 1), down_w[at, part:depth])
        gate = gate_b[:, at]
        sigmoid = jax.nn.sigmoid(gate)
        gate_g[:, at] = (hidden_grad * up_b[:, at] * (sigmoid * (1.0 + gate * (1.0 - sigmoid)))).astype(BF16)
        up_g[:, at] = (hidden_grad * (gate * sigmoid)).astype(BF16)

    sent(gather_b)
    for h in (0, 1):

        @pl.loop(0, part // tile)
        def _(i):
            at = pl.ds(pl.multiple_of(h * part + i * tile, tile), tile)
            back = dot_nt(gate_g[...], gate_w[at, :]) + dot_nt(up_g[...], up_w[at, :])
            tab_b[h, :, :, columns(i)] = back.astype(BF16).reshape(SIDE, SIDE * CAP, tile)

        if h == 0:
            last(gather_a)
        scatter_0(scatter_b, h)

    received(gather_a, "last")

    @pl.loop(0, steps)
    def _(i):
        gate = project(tab_a, gate_w, i)
        up = project(tab_a, up_w, i)
        hidden[:, columns(i)] = (gate * jax.nn.sigmoid(gate) * up).astype(BF16)

        @pl.when(i == 0)
        def _():
            scatter_1(scatter_b, tab_b, 0)

    sent(gather_c)
    for h in (0, 1):

        @pl.loop(0, part // tile)
        def _(i):
            at = pl.ds(pl.multiple_of(h * part + i * tile, tile), tile)
            out = dot(hidden[...], down_w[:, at])
            tab_c[h, :, :, columns(i)] = out.astype(BF16).reshape(SIDE, SIDE * CAP, tile)

        scatter_0(scatter_a, h)

    scatter_2(scatter_b, tab_b, 0)
    scatter_1(scatter_a, tab_c, 1)
    scatter_3(scatter_b, tab_b, 0)
    scatter_2(scatter_a, tab_c, 1)
    scatter_4(scatter_b, tab_b, 0)

    chunk = tokens // 4

    @pl.loop(0, 4)
    def _(i):
        at = pl.ds(pl.multiple_of(i * chunk, chunk), chunk)
        values = saved[at, :].astype(F32)
        scale = lax.rsqrt(jnp.mean(values * values, axis=-1, keepdims=True) + EPSILON)
        weighted = dot(place_b[at, :], rows_out[0]) * gain_ref[...]
        average = jnp.mean(weighted * values, axis=-1, keepdims=True)
        grad = cot[at, :].astype(F32) + scale * (weighted - values * scale * scale * average)
        cot[at, :] = grad.astype(BF16)

    write_grad = pltpu.make_async_copy(cot, grad_out.at[0], local_sem.at[4])
    write_grad.start()
    scatter_3(scatter_a, tab_c, 1)
    scatter_4(scatter_a, tab_c, 1)

    @pl.loop(0, 4)
    def _(i):
        at = pl.ds(pl.multiple_of(i * chunk, chunk), chunk)
        out = dot(place_a[at, :], rows_out[1])
        x_here[at, :] = (x_here[at, :].astype(F32) + cols[at, :] * out).astype(BF16)

    write_mixed = pltpu.make_async_copy(x_here, mixed_out.at[0], local_sem.at[5])
    write_mixed.start()
    sent(gather_a)
    sent(scatter_b)
    sent(scatter_a)
    copy_x.wait_send()
    copy_dy.wait_send()
    write_grad.wait()
    write_mixed.wait()


def routing(expert_ids, gate_values):
    chosen = expert_ids == 0
    flag = jnp.any(chosen, axis=1).astype(F32)
    return flag, jnp.sum(jnp.where(chosen, gate_values, 0.0), axis=1)


def shards(sections, x_in, ids_a, gates_a, x_saved, ids_b, gates_b, dy_in, gain, w_gate, w_up, w_down):
    route = jnp.stack(routing(ids_a[0], gates_a[0]) + routing(ids_b[0], gates_b[0]))
    route = jnp.concatenate([route, jnp.zeros_like(route)], axis=0)
    _, tokens, depth = x_in.shape
    width = w_gate.shape[2]
    rows, part = SIDE * SIDE * CAP, depth // 2
    copies = 2 + 3 * 20 + 2 * 24
    table = pltpu.VMEM((2, SIDE, SIDE * CAP, part), BF16)
    flops = 8 * 2 * rows * depth * width
    anywhere, vmem = pl.BlockSpec(memory_space=pl.ANY), pl.BlockSpec(memory_space=pltpu.VMEM)
    return pl.pallas_call(
        functools.partial(kernel, sections),
        out_shape=[jax.ShapeDtypeStruct(x_in.shape, BF16)] * 2,
        in_specs=[vmem, vmem] + [anywhere] * 6,
        out_specs=[anywhere] * 2,
        scratch_shapes=[
            pltpu.VMEM((depth, width), BF16),
            pltpu.VMEM((depth, width), BF16),
            pltpu.VMEM((width, depth), BF16),
            table, table, table,
            pltpu.VMEM((rows, width), F32),
            pltpu.VMEM((rows, width), F32),
            pltpu.VMEM((rows, width), BF16),
            pltpu.VMEM((rows, width), BF16),
            pltpu.VMEM((rows, width), BF16),
            pltpu.VMEM((tokens, depth), BF16),
            pltpu.VMEM((tokens, depth), BF16),
            pltpu.VMEM((tokens, depth), BF16),
            pltpu.VMEM((2, 2, 2, CAP, part), BF16),
            pltpu.VMEM((2, 2, 2 * CAP, part), BF16),
            pltpu.VMEM((2, 2, SIDE, CAP, part), BF16),
            pltpu.VMEM((2, 2, SIDE * CAP, part), BF16),
            pltpu.VMEM((2, 2, 2, CAP // 2, part), BF16),
            pltpu.VMEM((2, 2, 2, CAP, part), BF16),
            pltpu.VMEM((tokens, CAP), BF16),
            pltpu.VMEM((tokens, CAP), BF16),
            pltpu.VMEM((tokens, 1), F32),
            pltpu.VMEM((2, CAP, depth), BF16),
            pltpu.SemaphoreType.DMA((copies,)),
            pltpu.SemaphoreType.DMA((copies,)),
            pltpu.SemaphoreType.DMA((6,)),
        ],
        compiler_params=pltpu.CompilerParams(
            collective_id=0, has_side_effects=True, vmem_limit_bytes=60 * 1024 * 1024
        ),
        cost_estimate=pl.CostEstimate(
            flops=flops, bytes_accessed=3 * depth * width * 2 + 5 * tokens * depth * 2, transcendentals=2 * rows * width
        ),
    )(route, gain, x_in, x_saved, dy_in, w_gate, w_up, w_down)


def solution(mesh):
    tokens = P("section", "ed", None)
    return jax.shard_map(
        functools.partial(shards, mesh.shape["section"]),
        mesh=mesh,
        in_specs=(tokens,) * 7
        + (P("section", None), P("section", None, "ed"), P("section", None, "ed"), P("section", "ed", None)),
        out_specs=(tokens, tokens),
        check_vma=False,
    )
```

time: 390 us -> 137 us (0.35)
  waiting for transfers between devices: 288 us -> 0 us
  Pallas kernels: 0 us -> 126 us
  matrix products: 60.4 us -> 0 us
  between operations: 14 us -> 0.65 us
  other arithmetic: 12.1 us -> 2.83 us
  local copies, waits for them, and re-layouts: 11.9 us -> 5.19 us
    reduce_scatter x2 -> x0, waiting for transfers between devices: 142 us -> none  [the longest x1 73.9 us: shards(): lax.psum_scatter(fwd_terms.astype(jnp.bfloat16), 'ed', scatter_dimension=...]
    pallas_call x0 -> x1, Pallas kernels: none -> 126 us  [shards(): pl.pallas_call(functools.partial(kernel, sections), out_shape=[jax.ShapeD...]
    all_gather x2 -> x0, waiting for transfers between devices: 124 us -> none  [the longest x1 73.2 us: shards(): segment = lax.all_gather(stacked, 'ed', axis=0, tiled=True)]
    dot_general x7 -> x0, matrix products: 60.4 us -> none  [the longest x1 17 us: shards(): fwd_terms = jnp.dot(hidden, down_slice, preferred_element_type=jnp.float32)]
    ppermute x2 -> x0, waiting for transfers between devices: 22 us -> none  [from_behind(): return lax.ppermute(value, axis, pairs)]
    convert_element_type x7 -> x1, other arithmetic: 7.25 us -> 0.01 us  [routing(): flag = jnp.any(chosen, axis=1).astype(F32)]
    gather x5 -> x0, local copies, waits for them, and re-layouts: 6.83 us -> none  [the longest x1 3.04 us: shards(): send_fwd = padded(normed_a)[token_of_a]]
  transfers between devices with their start and end apart: 6 -> 0, of which waited for: 6 -> 0; matrix products, arithmetic and copies ran while one was open for 2% -> 0% of each run, Pallas kernels for 0% -> 0%
where the time goes in v1:
time: 137 us; the launch traced here: 134 us
  Pallas kernels  126 us (92%)
  local copies, waits for them, and re-layouts  5.19 us (4%)
  other arithmetic  2.83 us (2%)
    pallas_call x1, Pallas kernels, shards(): pl.pallas_call(functools.partial(kernel, sections), out_shape=[jax.ShapeD...  126 us
    unnamed x2, local copies, waits for them, and re-layouts  4.57 us

profile of v1, /device:TPU:0, one launch (start us, length us, event | category | flops | bytes accessed | tf_op | source)
XLA Modules:
  0.0 134.4 jit_solution(5068286743888778766)
XLA Ops:
  0.6 0.7 select_reduce_fusion.1
  1.3 0.7 select_reduce_fusion
  2.1 0.7 fusion
  2.8 0.7 fusion.1
  3.5 0.6 concatenate.3.route_ref
  4.1 125.7 %shard_map.122 = (bf16[1,128,4096]{2,1,0:T(8,128)(2,1)}, bf16[1,128,4096]{2,1,0:T(8,128)(2,1)}) custom-call(f32[8,128]{1,0:T(8,128)} %concatenate.3.route_ref, f32[1,4096]{1,0:T(1,128)} %gain_ref.1, bf16[1,128,4096]{2,1,0:T(8,128)(2,1)} %x_in.1, bf16[1,128,4096]{2,1,0:T(8,128)(2,1)} %x_saved.1, bf16[1,128,4096]{2,1,0:T(8,128)(2,1)} %dy_in.1, ...), custom_call_target="tpu_custom_call" | custom-call | flops 25769803776 | bytes 24117248 | tf_op jit(solution)/shard_map/pallas_call | solution.py:412
  129.8 2.3 %copy.15 = bf16[1,128,4096]{2,1,0:T(8,128)(2,1)} copy(bf16[1,128,4096]{2,1,0:T(8,128)(2,1)} %get-tuple-element.6) | data formatting | bytes 2097152
  132.1 2.3 %copy.16 = bf16[1,128,4096]{2,1,0:T(8,128)(2,1)} copy(bf16[1,128,4096]{2,1,0:T(8,128)(2,1)} %get-tuple-element.7) | data formatting | bytes 2097152
  (2 shorter events, 0.0 us)

commit v2 on v1

v2 whole, which is shorter than its diff:
```python
import functools

import jax
import jax.numpy as jnp
from jax import lax
from jax.experimental import pallas as pl
from jax.experimental.pallas import tpu as pltpu
from jax.sharding import PartitionSpec as P

EPSILON = 1e-06
MESH = pl.DeviceIdType.MESH
SIDE = 4
CAP = 32
PLUS, MINUS = 0, 1
PLAN = {
    "early": ('b1', 'b2', 'dy', 'c0', 'b3', 'c1', 'b4', 'x', 'c2', 'b5', 'c3', 'a0'),
    "project b": {0: ('c4',), 1: ('a1',)},
    "before hidden": ('c5',),
    "hidden grad": {0: ('a2',), 2: ('a3',)},
    "back 0": {4: ('a4',)},
    "back 1": {},
    "before project a": ("a5",),
    "project a": {1: ("sb1",)},
    "down 0": {},
    "down 1": {},
}
F32, BF16 = jnp.float32, jnp.bfloat16
NT = (((1,), (1,)), ((), ()))


def dot(a, b):
    return jnp.dot(a, b, preferred_element_type=F32)


def dot_nt(a, b):
    return lax.dot_general(a, b, NT, preferred_element_type=F32)


def group(table, half, first, second):
    low, high = first
    if half == 0:
        return table.at[0, low:high, second * CAP : (second + 1) * CAP]
    return table.at[1, second, low * CAP : high * CAP]


def rows_of(table, half, first, rows):
    low, high = rows
    if half == 0:
        return table.at[0, first, low:high]
    return table.at[1, 0, first * CAP + low : first * CAP + high]


def flag_and_share(ids, gates):
    chosen = ids[...] == 0
    return (
        jnp.sum(jnp.where(chosen, 1.0, 0.0), axis=0, keepdims=True),
        jnp.sum(jnp.where(chosen, gates[...], 0.0), axis=0, keepdims=True),
    )


def column(row):
    n = row.shape[1]
    rows, columns = lax.broadcasted_iota(jnp.int32, (n, n), 0), lax.broadcasted_iota(jnp.int32, (n, n), 1)
    return jnp.sum(jnp.where(rows == columns, row, 0.0), axis=1, keepdims=True)


def slot_code(flag):
    n = flag.shape[1]
    rows, columns = lax.broadcasted_iota(jnp.int32, (n, n), 0), lax.broadcasted_iota(jnp.int32, (n, n), 1)
    count = jnp.sum(jnp.where(rows <= columns, column(flag), 0.0), axis=0, keepdims=True)
    return jnp.where(flag > 0.5, count - 1.0, -1.0)


def kernel(
    sections,
    ids_a, gates_a, ids_b, gates_b, gain_ref, x_in, x_saved, dy_in, w_gate, w_up, w_down,
    x_out, grad_out, rows_a_out,
    gate_w, up_w, down_w, tab_b, tab_c, tab_a,
    gate_b, up_b, gate_g, up_g, hidden,
    x_here, saved, cot,
    acc_s0, acc_s1, fin_s0, fin_s1, acc_f, fin_f,
    place_b, rows_out,
    send_sem, recv_sem, local_sem,
):
    section, ed = lax.axis_index("section"), lax.axis_index("ed")
    x, z = ed // SIDE, ed % SIDE

    def at_x(step):
        return (section, (x + step + SIDE) % SIDE * SIDE + z)

    def at_z(step):
        return (section, x * SIDE + (z + step + SIDE) % SIDE)

    def at_section(step):
        return ((section + step + sections) % sections, ed)

    counter = [0]

    def remote(src, dst, device):
        k = counter[0]
        counter[0] += 1
        return pltpu.make_async_remote_copy(
            src_ref=src, dst_ref=dst, send_sem=send_sem.at[k], recv_sem=recv_sem.at[k],
            device_id=device, device_id_type=MESH,
        )

    def along(half, which, direction):
        step = 1 if direction == PLUS else -1
        on_x = (which == "f") == (half == 0)
        return at_x(step) if on_x else at_z(step)

    width = gate_w.shape[1]
    depth = gate_w.shape[0]
    part = depth // 2
    rows = SIDE * SIDE * CAP
    tokens = saved.shape[0]
    tile = min(256, width)
    half_rows = CAP // 2
    low_rows, high_rows = (0, half_rows), (half_rows, CAP)

    def gather_copies(table):
        made = {}
        for h in (0, 1):
            for d in (PLUS, MINUS):
                back = 2 if d == PLUS else 1
                rows_here = low_rows if d == PLUS else high_rows
                first = 0 if d == PLUS else 2
                f, s = along(h, "f", d), along(h, "s", d)
                made[h, d, "near"] = remote(group(table, h, (0, 1), 0), group(table, h, (back, back + 1), 0), f)
                made[h, d, "own"] = remote(group(table, h, (0, 1), 0), group(table, h, (0, 1), back), s)
                made[h, d, "far"] = remote(rows_of(table, h, back, rows_here), rows_of(table, h, 3, rows_here), f)
                made[h, d, "beside"] = remote(group(table, h, (1, 3), 0), group(table, h, (1, 3), back), s)
                made[h, d, "across"] = remote(group(table, h, (3, 4), 0), group(table, h, (3, 4), back), s)
                for name, p in (("pass_0", first), ("pass_1", first + 1)):
                    made[h, d, name] = remote(group(table, h, (p, p + 1), back), group(table, h, (p, p + 1), 3), s)
        return made

    def fin_slice(t, half, direction, pair):
        low, high = pair
        if half == 0:
            return fin_s0.at[t, direction, low:high]
        return fin_s1.at[t, direction, low * CAP : high * CAP]

    def acc_slice(t, half, direction, low):
        if half == 0:
            return acc_s0.at[t, direction, low : low + 1]
        return acc_s1.at[t, direction, low * CAP : (low + 1) * CAP]

    def scatter_copies(table, t):
        made = {}
        for h in (0, 1):
            acc = acc_s0 if h == 0 else acc_s1
            for d in (PLUS, MINUS):
                near = 1 if d == PLUS else 2
                mine, other = ((0, 2), (2, 4)) if d == PLUS else ((2, 4), (0, 2))
                my_rows, other_rows = (low_rows, high_rows) if d == PLUS else (high_rows, low_rows)
                f, s = along(h, "f", d), along(h, "s", d)
                made[h, d, "sa"] = remote(group(table, h, mine, 3), acc.at[t, d], s)
                made[h, d, "sd"] = remote(group(table, h, other, near), fin_slice(t, h, d, other), s)
                for name, p in (("sf_0", mine[0] + 1), ("sf_1", mine[0])):
                    made[h, d, name] = remote(group(table, h, (p, p + 1), near), fin_slice(t, h, d, (p, p + 1)), s)
                made[h, d, "fa"] = remote(rows_of(table, h, 3, my_rows), acc_f.at[t, h, d], f)
                made[h, d, "fd"] = remote(
                    rows_of(table, h, near, other_rows), fin_f.at[t, h, d, other_rows[0] : other_rows[1]], f
                )
                made[h, d, "ff"] = remote(
                    rows_of(table, h, near, my_rows), fin_f.at[t, h, d, my_rows[0] : my_rows[1]], f
                )
        return made

    both = [(h, d) for h in (0, 1) for d in (PLUS, MINUS)]
    copy_x = remote(x_in.at[0], x_here, at_section(1))
    copy_dy = remote(dy_in.at[0], cot, at_section(-1))
    gather_b, gather_c, gather_a = gather_copies(tab_b), gather_copies(tab_c), gather_copies(tab_a)
    scatter_b, scatter_a = scatter_copies(tab_b, 0), scatter_copies(tab_c, 1)

    def sent(copies):
        for copy in copies.values():
            copy.wait_send()

    def gather_0(copies):
        for name in ("near", "own"):
            for h, d in both:
                copies[h, d, name].start()

    def gather_1(copies):
        for h in (0, 1):
            for d in (PLUS, MINUS):
                copies[h, d, "near"].wait_recv()
                copies[h, d, "far"].start()
            for d in (PLUS, MINUS):
                copies[h, d, "beside"].start()

    def gather_2(copies):
        for h in (0, 1):
            for d in (PLUS, MINUS):
                copies[h, d, "far"].wait_recv()
            for d in (PLUS, MINUS):
                copies[h, d, "across"].start()
                copies[h, d, "own"].wait_recv()
            copies[h, PLUS, "pass_0"].start()

    def gather_3(copies):
        for h, d in both:
            copies[h, d, "beside"].wait_recv()
            copies[h, d, "pass_1" if d == PLUS else "pass_0"].start()

    def gather_4(copies):
        for h, d in both:
            copies[h, d, "across"].wait_recv()
            if d == MINUS:
                copies[h, d, "pass_1"].start()

    def gather_5(copies):
        for h, d in both:
            copies[h, d, "pass_0"].wait_recv()
            copies[h, d, "pass_1"].wait_recv()

    def scatter_0(copies, h):
        for name in ("sa", "sd"):
            for d in (PLUS, MINUS):
                copies[h, d, name].start()

    def add_into(target, other):
        target[...] = (target[...].astype(F32) + other[...].astype(F32)).astype(BF16)

    def scatter_1(copies, table, t):
        for h in (0, 1):
            for d in (PLUS, MINUS):
                copies[h, d, "sa"].wait_recv()
            for name, offset in (("sf_0", 1), ("sf_1", 0)):
                for d in (PLUS, MINUS):
                    near, p = (1, offset) if d == PLUS else (2, 2 + offset)
                    add_into(group(table, h, (p, p + 1), near), acc_slice(t, h, d, offset))
                    copies[h, d, name].start()

    def total(table, t, h, p):
        target = group(table, h, (p, p + 1), 0)
        one, two = fin_slice(t, h, PLUS, (p, p + 1)), fin_slice(t, h, MINUS, (p, p + 1))
        target[...] = (target[...].astype(F32) + one[...].astype(F32) + two[...].astype(F32)).astype(BF16)

    def scatter_2(copies, table, t):
        for h in (0, 1):
            for d in (PLUS, MINUS):
                copies[h, d, "sd"].wait_recv()
                copies[h, d, "sf_0"].wait_recv()
            total(table, t, h, 3)
            for d in (PLUS, MINUS):
                copies[h, d, "fa"].start()
            total(table, t, h, 1)
            copies[h, PLUS, "fd"].start()
        for h in (0, 1):
            copies[h, MINUS, "sf_1"].wait_recv()
            total(table, t, h, 2)
            copies[h, MINUS, "fd"].start()

    def scatter_3(copies, table, t):
        for h, d in both:
            near = 1 if d == PLUS else 2
            my_rows = low_rows if d == PLUS else high_rows
            copies[h, d, "fa"].wait_recv()
            add_into(rows_of(table, h, near, my_rows), acc_f.at[t, h, d])
            copies[h, d, "ff"].start()

    def scatter_own(copies, table, t):
        for h in (0, 1):
            copies[h, PLUS, "sf_1"].wait_recv()
            total(table, t, h, 0)

    def scatter_4(copies, table, t):
        for h in (0, 1):
            for d in (PLUS, MINUS):
                copies[h, d, "fd"].wait_recv()
                copies[h, d, "ff"].wait_recv()
            out = (
                rows_of(table, h, 0, (0, CAP))[...].astype(F32)
                + fin_f[t, h, PLUS].astype(F32)
                + fin_f[t, h, MINUS].astype(F32)
            )
            rows_out[t, :, h * part : (h + 1) * part] = out.astype(BF16)

    load_saved = pltpu.make_async_copy(x_saved.at[0], saved, local_sem.at[0])
    load_saved.start()
    loads = [
        pltpu.make_async_copy(src.at[0], dst, local_sem.at[k])
        for k, (src, dst) in enumerate(((w_gate, gate_w), (w_up, up_w), (w_down, down_w)), start=1)
    ]
    keep_x = pltpu.make_async_copy(x_here, x_out, local_sem.at[6])
    barrier = pltpu.get_barrier_semaphore()
    for device in (at_x(1), at_x(-1), at_z(1), at_z(-1), at_section(1), at_section(-1)):
        pl.semaphore_signal(barrier, inc=1, device_id=device, device_id_type=MESH)

    flag_a, share_a = flag_and_share(ids_a, gates_a)
    flag_b, share_b = flag_and_share(ids_b, gates_b)
    slot_rows = lax.broadcasted_iota(jnp.int32, (CAP, tokens), 0).astype(F32)
    slot_cols = lax.broadcasted_iota(jnp.int32, (tokens, CAP), 1).astype(F32)
    code_b = slot_code(flag_b)
    take_a = jnp.where(slot_code(flag_a) == slot_rows, 1.0, 0.0).astype(BF16)
    take_b = jnp.where(code_b == slot_rows, 1.0, 0.0)
    share_slot = jnp.sum(take_b * share_b, axis=1, keepdims=True)
    take_b = take_b.astype(BF16)
    place_b[...] = jnp.where(column(code_b) == slot_cols, 1.0, 0.0).astype(BF16)

    pl.semaphore_wait(barrier, 6)
    copy_x.start()
    copy_dy.start()

    def put_own(table, values):
        for h in (0, 1):
            table[h, 0, 0:CAP, :] = values[:, h * part : (h + 1) * part]

    def normed(values):
        scale = lax.rsqrt(jnp.mean(values * values, axis=-1, keepdims=True) + EPSILON)
        return (values * scale * gain_ref[...]).astype(BF16)

    load_saved.wait()
    put_own(tab_b, normed(dot(take_b, saved[...])))
    def rows_c():
        copy_dy.wait_recv()
        put_own(tab_c, (share_slot * dot(take_b, cot[...])).astype(BF16))

    def rows_a():
        copy_x.wait_recv()
        keep_x.start()
        put_own(tab_a, normed(dot(take_a, x_here[...])))

    gather = (gather_0, gather_1, gather_2, gather_3, gather_4, gather_5)
    steps = {"dy": rows_c, "x": rows_a}
    for name, copies in (("a", gather_a), ("b", gather_b), ("c", gather_c)):
        for k, step in enumerate(gather):
            steps[f"{name}{k}"] = functools.partial(step, copies)
    scatter = {1: scatter_1, 2: scatter_2, 3: scatter_3, 4: scatter_4, 5: scatter_own}
    for name, copies, table, t in (("a", scatter_a, tab_c, 1), ("b", scatter_b, tab_b, 0)):
        for k, step in scatter.items():
            steps[f"s{name}{k}"] = functools.partial(step, copies, table, t)

    def do(*names):
        for name in names:
            steps[name]()

    def during(label, i):
        for k, names in PLAN[label].items():

            @pl.when(i == k)
            def _():
                do(*names)

    do("b0")
    for load in loads:
        load.start()
    do(*PLAN["early"])
    for load in loads:
        load.wait()

    def tall(table, h):
        return table[h].reshape(rows, part)

    def columns(i):
        return pl.ds(pl.multiple_of(i * tile, tile), tile)

    def project(table, weight, i):
        return dot(tall(table, 0), weight[0:part, columns(i)]) + dot(tall(table, 1), weight[part:depth, columns(i)])

    count = width // tile

    @pl.loop(0, count)
    def _(i):
        gate_b[:, columns(i)] = project(tab_b, gate_w, i)
        up_b[:, columns(i)] = project(tab_b, up_w, i)
        during("project b", i)

    do(*PLAN["before hidden"])

    @pl.loop(0, count)
    def _(i):
        at = columns(i)
        hidden_grad = dot_nt(tall(tab_c, 0), down_w[at, 0:part]) + dot_nt(tall(tab_c, 1), down_w[at, part:depth])
        gate = gate_b[:, at]
        sigmoid = jax.nn.sigmoid(gate)
        gate_g[:, at] = (hidden_grad * up_b[:, at] * (sigmoid * (1.0 + gate * (1.0 - sigmoid)))).astype(BF16)
        up_g[:, at] = (hidden_grad * (gate * sigmoid)).astype(BF16)
        during("hidden grad", i)

    sent(gather_b)
    for h in (0, 1):

        @pl.loop(0, part // tile)
        def _(i):
            at = pl.ds(pl.multiple_of(h * part + i * tile, tile), tile)
            back = dot_nt(gate_g[...], gate_w[at, :]) + dot_nt(up_g[...], up_w[at, :])
            tab_b[h, :, :, columns(i)] = back.astype(BF16).reshape(SIDE, SIDE * CAP, tile)
            during(f"back {h}", i)

        scatter_0(scatter_b, h)

    do(*PLAN["before project a"])

    @pl.loop(0, count)
    def _(i):
        gate = project(tab_a, gate_w, i)
        up = project(tab_a, up_w, i)
        hidden[:, columns(i)] = (gate * jax.nn.sigmoid(gate) * up).astype(BF16)
        during("project a", i)

    sent(gather_c)
    for h in (0, 1):

        @pl.loop(0, part // tile)
        def _(i):
            at = pl.ds(pl.multiple_of(h * part + i * tile, tile), tile)
            out = dot(hidden[...], down_w[:, at])
            tab_c[h, :, :, columns(i)] = out.astype(BF16).reshape(SIDE, SIDE * CAP, tile)
            during(f"down {h}", i)

        scatter_0(scatter_a, h)

    scatter_2(scatter_b, tab_b, 0)
    scatter_1(scatter_a, tab_c, 1)
    scatter_3(scatter_b, tab_b, 0)
    scatter_own(scatter_b, tab_b, 0)
    scatter_2(scatter_a, tab_c, 1)
    scatter_4(scatter_b, tab_b, 0)

    chunk = tokens // 4

    def grad_part(i):
        at = pl.ds(pl.multiple_of(i * chunk, chunk), chunk)
        values = saved[at, :].astype(F32)
        scale = lax.rsqrt(jnp.mean(values * values, axis=-1, keepdims=True) + EPSILON)
        weighted = dot(place_b[at, :], rows_out[0]) * gain_ref[...]
        average = jnp.mean(weighted * values, axis=-1, keepdims=True)
        grad = cot[at, :].astype(F32) + scale * (weighted - values * scale * scale * average)
        cot[at, :] = grad.astype(BF16)

    pl.loop(0, 2)(grad_part)
    scatter_3(scatter_a, tab_c, 1)
    pl.loop(2, 4)(grad_part)
    write_grad = pltpu.make_async_copy(cot, grad_out, local_sem.at[4])
    write_grad.start()
    scatter_own(scatter_a, tab_c, 1)
    scatter_4(scatter_a, tab_c, 1)
    write_rows = pltpu.make_async_copy(rows_out.at[1], rows_a_out, local_sem.at[5])
    write_rows.start()
    sent(gather_a)
    sent(scatter_b)
    sent(scatter_a)
    copy_x.wait_send()
    copy_dy.wait_send()
    keep_x.wait()
    write_grad.wait()
    write_rows.wait()


def finish(ids_a, gates_a, x_here, rows_a, grad, mixed_out, grad_out, x_part, grad_part, rows, sem):
    tokens = x_part.shape[0]
    chunk = tokens // 4
    load_rows = pltpu.make_async_copy(rows_a, rows, sem.at[8])
    load_rows.start()
    chunks = [pl.ds(i * chunk, chunk) for i in range(4)]
    wide = x_part.shape[1] // 4
    strips = [pl.ds(i * wide, wide) for i in range(4)]
    loads = [pltpu.make_async_copy(x_here.at[:, at], x_part.at[:, at], sem.at[i]) for i, at in enumerate(strips)]
    takes = [pltpu.make_async_copy(grad.at[at], grad_part.at[at], sem.at[4 + i]) for i, at in enumerate(chunks)]
    for copy in loads + takes:
        copy.start()
    flag, share = flag_and_share(ids_a, gates_a)
    place = (column(slot_code(flag)) == lax.broadcasted_iota(jnp.int32, (tokens, CAP), 1).astype(F32)).astype(F32)
    place = place.astype(BF16)
    share = column(share)
    load_rows.wait()
    writes = []
    for i, (at, strip) in enumerate(zip(chunks, strips)):
        loads[i].wait()
        x_part[:, strip] = (x_part[:, strip].astype(F32) + share * dot(place, rows[:, strip])).astype(BF16)
        writes.append(pltpu.make_async_copy(x_part.at[:, strip], mixed_out.at[0, :, strip], sem.at[9 + i]))
        writes[-1].start()
        takes[i].wait()
        writes.append(pltpu.make_async_copy(grad_part.at[at], grad_out.at[0, at], sem.at[13 + i]))
        writes[-1].start()
    for write in writes:
        write.wait()


def shards(sections, x_in, ids_a, gates_a, x_saved, ids_b, gates_b, dy_in, gain, w_gate, w_up, w_down):
    _, tokens, depth = x_in.shape
    width = w_gate.shape[2]
    rows, part = SIDE * SIDE * CAP, depth // 2
    copies = 2 + 3 * 28 + 2 * 28
    table = pltpu.VMEM((2, SIDE, SIDE * CAP, part), BF16)
    flops = 8 * 2 * rows * depth * width
    anywhere, vmem = pl.BlockSpec(memory_space=pl.ANY), pl.BlockSpec(memory_space=pltpu.VMEM)
    block = jax.ShapeDtypeStruct((tokens, depth), BF16)
    routes = ids_a[0].T, gates_a[0].T, ids_b[0].T, gates_b[0].T
    x_here, grad, rows_a = pl.pallas_call(
        functools.partial(kernel, sections),
        out_shape=[block, block, jax.ShapeDtypeStruct((CAP, depth), BF16)],
        in_specs=[vmem] * 5 + [anywhere] * 6,
        out_specs=[anywhere] * 3,
        scratch_shapes=[
            pltpu.VMEM((depth, width), BF16),
            pltpu.VMEM((depth, width), BF16),
            pltpu.VMEM((width, depth), BF16),
            table, table, table,
            pltpu.VMEM((rows, width), F32),
            pltpu.VMEM((rows, width), F32),
            pltpu.VMEM((rows, width), BF16),
            pltpu.VMEM((rows, width), BF16),
            pltpu.VMEM((rows, width), BF16),
            pltpu.VMEM((tokens, depth), BF16),
            pltpu.VMEM((tokens, depth), BF16),
            pltpu.VMEM((tokens, depth), BF16),
            pltpu.VMEM((2, 2, 2, CAP, part), BF16),
            pltpu.VMEM((2, 2, 2 * CAP, part), BF16),
            pltpu.VMEM((2, 2, SIDE, CAP, part), BF16),
            pltpu.VMEM((2, 2, SIDE * CAP, part), BF16),
            pltpu.VMEM((2, 2, 2, CAP // 2, part), BF16),
            pltpu.VMEM((2, 2, 2, CAP, part), BF16),
            pltpu.VMEM((tokens, CAP), BF16),
            pltpu.VMEM((2, CAP, depth), BF16),
            pltpu.SemaphoreType.DMA((copies,)),
            pltpu.SemaphoreType.DMA((copies,)),
            pltpu.SemaphoreType.DMA((7,)),
        ],
        compiler_params=pltpu.CompilerParams(
            collective_id=0, has_side_effects=True, vmem_limit_bytes=60 * 1024 * 1024
        ),
        cost_estimate=pl.CostEstimate(
            flops=flops, bytes_accessed=3 * depth * width * 2 + 5 * tokens * depth * 2, transcendentals=2 * rows * width
        ),
    )(*routes, gain, x_in, x_saved, dy_in, w_gate, w_up, w_down)
    return pl.pallas_call(
        finish,
        out_shape=[jax.ShapeDtypeStruct(x_in.shape, BF16)] * 2,
        in_specs=[vmem] * 2 + [anywhere] * 3,
        out_specs=[anywhere] * 2,
        scratch_shapes=[
            pltpu.VMEM((tokens, depth), BF16),
            pltpu.VMEM((tokens, depth), BF16),
            pltpu.VMEM((CAP, depth), BF16),
            pltpu.SemaphoreType.DMA((17,)),
        ],
        compiler_params=pltpu.CompilerParams(vmem_limit_bytes=60 * 1024 * 1024),
    )(routes[0], routes[1], x_here, rows_a, grad)


def solution(mesh):
    tokens = P("section", "ed", None)
    return jax.shard_map(
        functools.partial(shards, mesh.shape["section"]),
        mesh=mesh,
        in_specs=(tokens,) * 7
        + (P("section", None), P("section", None, "ed"), P("section", None, "ed"), P("section", "ed", None)),
        out_specs=(tokens, tokens),
        check_vma=False,
    )
```

time: 137 us -> 130 us (0.949); the launches traced: 134 us -> 129 us
  local copies, waits for them, and re-layouts: 5.19 us -> 0 us
  Pallas kernels: 126 us -> 129 us
  other arithmetic: 2.83 us -> 0 us
    unnamed x2 -> x0, local copies, waits for them, and re-layouts: 4.57 us -> none
    pallas_call x1 -> x2, Pallas kernels: 126 us -> 129 us  [the longest x1 125 us: shards(): pl.pallas_call(functools.partial(kernel, sections), out_shape=[block, blo...]
    reduce_sum x2 -> x0, other arithmetic: 1.43 us -> none  [routing(): return (flag, jnp.sum(jnp.where(chosen, gate_values, 0.0), axis=1))]
    reduce_or x2 -> x0, other arithmetic: 1.4 us -> none  [routing(): flag = jnp.any(chosen, axis=1).astype(F32)]
where the time goes in v2:
time: 130 us; the launch traced here: 129 us
  Pallas kernels  129 us (99%)
    pallas_call x1, Pallas kernels, shards(): pl.pallas_call(functools.partial(kernel, sections), out_shape=[block, blo...  125 us
    pallas_call x1, Pallas kernels, shards(): pl.pallas_call(finish, out_shape=[jax.ShapeDtypeStruct(x_in.shape, BF16)]...  3.61 us

profile of v2, /device:TPU:0, one launch (start us, length us, event | category | flops | bytes accessed | tf_op | source)
XLA Modules:
  0.0 129.4 jit_solution(440728611357842277)
XLA Ops:
  0.6 125.2 %shard_map.122 = (bf16[128,4096]{1,0:T(8,128)(2,1)}, bf16[128,4096]{1,0:T(8,128)(2,1)}, bf16[32,4096]{1,0:T(8,128)(2,1)}) custom-call(s32[2,128]{1,0:T(2,128)} %bitcast.12, f32[2,128]{1,0:T(2,128)} %bitcast.14, s32[2,128]{1,0:T(2,128)} %bitcast.16, f32[2,128]{1,0:T(2,128)} %bitcast.17, f32[1,4096]{1,0:T(1,128)} %gain_ref.1, bf16[1,128,4096]{2,1,0:T(8,128)(2,1)} %x_in.1, ...), custom_call_target="tpu_custom_call" | custom-call | flops 25769803776 | bytes 24117248 | tf_op jit(solution)/shard_map/pallas_call | solution.py:494
  125.8 3.6 %shard_map.123 = (bf16[1,128,4096]{2,1,0:T(8,128)(2,1)}, bf16[1,128,4096]{2,1,0:T(8,128)(2,1)}) custom-call(s32[2,128]{1,0:T(2,128)} %bitcast.13, f32[2,128]{1,0:T(2,128)} %bitcast.15, bf16[128,4096]{1,0:T(8,128)(2,1)} %get-tuple-element.5.x_here, bf16[32,4096]{1,0:T(8,128)(2,1)} %get-tuple-element.6.rows_a, bf16[128,4096]{1,0:T(8,128)(2,1)} %get-tuple-element.7.grad), custom_call_target="tpu_custom_call" | custom-call | tf_op jit(solution)/shard_map/pallas_call | solution.py:531

commit v3 on v2

--- a/solution.py
+++ b/solution.py
@@ -13,11 +13,11 @@
 CAP = 32
 PLUS, MINUS = 0, 1
 PLAN = {
-    "early": ('b1', 'b2', 'dy', 'c0', 'b3', 'c1', 'b4', 'x', 'c2', 'b5', 'c3', 'a0'),
-    "project b": {0: ('c4',), 1: ('a1',)},
-    "before hidden": ('c5',),
-    "hidden grad": {0: ('a2',), 2: ('a3',)},
-    "back 0": {4: ('a4',)},
+    "early": ("b1", "b2", "dy", "c0", "b3", "c1", "b4", "c2", "x", "b5", "c3", "a0", "c4"),
+    "project b": {0: ("a1",)},
+    "before hidden": ("c5",),
+    "hidden grad": {0: ("a2",), 1: ("a3",)},
+    "back 0": {0: ("a4",)},
     "back 1": {},
     "before project a": ("a5",),
     "project a": {1: ("sb1",)},
@@ -73,14 +73,14 @@
 
 def kernel(
     sections,
-    ids_a, gates_a, ids_b, gates_b, gain_ref, x_in, x_saved, dy_in, w_gate, w_up, w_down,
+    ids_a_in, gates_a_in, ids_b_in, gates_b_in, gain_in, x_in, x_saved, dy_in, w_gate, w_up, w_down,
     x_out, grad_out, rows_a_out,
     gate_w, up_w, down_w, tab_b, tab_c, tab_a,
     gate_b, up_b, gate_g, up_g, hidden,
     x_here, saved, cot,
     acc_s0, acc_s1, fin_s0, fin_s1, acc_f, fin_f,
-    place_b, rows_out,
-    send_sem, recv_sem, local_sem,
+    place_b, rows_out, ids_a, gates_a, ids_b, gates_b, gain_ref,
+    send_sem, recv_sem, local_sem, small_sem,
 ):
     section, ed = lax.axis_index("section"), lax.axis_index("ed")
     x, z = ed // SIDE, ed % SIDE
@@ -279,17 +279,27 @@
             )
             rows_out[t, :, h * part : (h + 1) * part] = out.astype(BF16)
 
+    barrier = pltpu.get_barrier_semaphore()
+    for device in (at_x(1), at_x(-1), at_z(1), at_z(-1), at_section(1), at_section(-1)):
+        pl.semaphore_signal(barrier, inc=1, device_id=device, device_id_type=MESH)
+    small = [
+        pltpu.make_async_copy(src, dst, small_sem.at[k])
+        for k, (src, dst) in enumerate(
+            ((ids_b_in, ids_b), (gates_b_in, gates_b), (ids_a_in, ids_a), (gates_a_in, gates_a), (gain_in, gain_ref))
+        )
+    ]
     load_saved = pltpu.make_async_copy(x_saved.at[0], saved, local_sem.at[0])
     load_saved.start()
+    for copy in small:
+        copy.start()
     loads = [
         pltpu.make_async_copy(src.at[0], dst, local_sem.at[k])
         for k, (src, dst) in enumerate(((w_gate, gate_w), (w_up, up_w), (w_down, down_w)), start=1)
     ]
     keep_x = pltpu.make_async_copy(x_here, x_out, local_sem.at[6])
-    barrier = pltpu.get_barrier_semaphore()
-    for device in (at_x(1), at_x(-1), at_z(1), at_z(-1), at_section(1), at_section(-1)):
-        pl.semaphore_signal(barrier, inc=1, device_id=device, device_id_type=MESH)
-
+
+    for copy in small:
+        copy.wait()
     flag_a, share_a = flag_and_share(ids_a, gates_a)
     flag_b, share_b = flag_and_share(ids_b, gates_b)
     slot_rows = lax.broadcasted_iota(jnp.int32, (CAP, tokens), 0).astype(F32)
@@ -301,9 +311,6 @@
     take_b = take_b.astype(BF16)
     place_b[...] = jnp.where(column(code_b) == slot_cols, 1.0, 0.0).astype(BF16)
 
-    pl.semaphore_wait(barrier, 6)
-    copy_x.start()
-    copy_dy.start()
 
     def put_own(table, values):
         for h in (0, 1):
@@ -345,6 +352,9 @@
             def _():
                 do(*names)
 
+    pl.semaphore_wait(barrier, 6)
+    copy_x.start()
+    copy_dy.start()
     do("b0")
     for load in loads:
         load.start()
@@ -355,8 +365,11 @@
     def tall(table, h):
         return table[h].reshape(rows, part)
 
+    def strip(i, size):
+        return pl.ds(pl.multiple_of(i * size, size), size)
+
     def columns(i):
-        return pl.ds(pl.multiple_of(i * tile, tile), tile)
+        return strip(i, tile)
 
     def project(table, weight, i):
         return dot(tall(table, 0), weight[0:part, columns(i)]) + dot(tall(table, 1), weight[part:depth, columns(i)])
@@ -371,9 +384,9 @@
 
     do(*PLAN["before hidden"])
 
-    @pl.loop(0, count)
+    @pl.loop(0, 2)
     def _(i):
-        at = columns(i)
+        at = strip(i, width // 2)
         hidden_grad = dot_nt(tall(tab_c, 0), down_w[at, 0:part]) + dot_nt(tall(tab_c, 1), down_w[at, part:depth])
         gate = gate_b[:, at]
         sigmoid = jax.nn.sigmoid(gate)
@@ -384,11 +397,11 @@
     sent(gather_b)
     for h in (0, 1):
 
-        @pl.loop(0, part // tile)
+        @pl.loop(0, 2)
         def _(i):
-            at = pl.ds(pl.multiple_of(h * part + i * tile, tile), tile)
+            at = strip(2 * h + i, part // 2)
             back = dot_nt(gate_g[...], gate_w[at, :]) + dot_nt(up_g[...], up_w[at, :])
-            tab_b[h, :, :, columns(i)] = back.astype(BF16).reshape(SIDE, SIDE * CAP, tile)
+            tab_b[h, :, :, strip(i, part // 2)] = back.astype(BF16).reshape(SIDE, SIDE * CAP, part // 2)
             during(f"back {h}", i)
 
         scatter_0(scatter_b, h)
@@ -405,11 +418,11 @@
     sent(gather_c)
     for h in (0, 1):
 
-        @pl.loop(0, part // tile)
+        @pl.loop(0, 2)
         def _(i):
-            at = pl.ds(pl.multiple_of(h * part + i * tile, tile), tile)
+            at = strip(2 * h + i, part // 2)
             out = dot(hidden[...], down_w[:, at])
-            tab_c[h, :, :, columns(i)] = out.astype(BF16).reshape(SIDE, SIDE * CAP, tile)
+            tab_c[h, :, :, strip(i, part // 2)] = out.astype(BF16).reshape(SIDE, SIDE * CAP, part // 2)
             during(f"down {h}", i)
 
         scatter_0(scatter_a, h)
@@ -451,11 +464,14 @@
     write_rows.wait()
 
 
-def finish(ids_a, gates_a, x_here, rows_a, grad, mixed_out, grad_out, x_part, grad_part, rows, sem):
+def finish(ids_in, gates_in, x_here, rows_a, grad, mixed_out, grad_out, ids_a, gates_a, x_part, grad_part, rows, sem):
     tokens = x_part.shape[0]
     chunk = tokens // 4
     load_rows = pltpu.make_async_copy(rows_a, rows, sem.at[8])
-    load_rows.start()
+    load_ids = pltpu.make_async_copy(ids_in, ids_a, sem.at[17])
+    load_gates = pltpu.make_async_copy(gates_in, gates_a, sem.at[18])
+    for copy in (load_ids, load_gates, load_rows):
+        copy.start()
     chunks = [pl.ds(i * chunk, chunk) for i in range(4)]
     wide = x_part.shape[1] // 4
     strips = [pl.ds(i * wide, wide) for i in range(4)]
@@ -463,6 +479,8 @@
     takes = [pltpu.make_async_copy(grad.at[at], grad_part.at[at], sem.at[4 + i]) for i, at in enumerate(chunks)]
     for copy in loads + takes:
         copy.start()
+    load_ids.wait()
+    load_gates.wait()
     flag, share = flag_and_share(ids_a, gates_a)
     place = (column(slot_code(flag)) == lax.broadcasted_iota(jnp.int32, (tokens, CAP), 1).astype(F32)).astype(F32)
     place = place.astype(BF16)
@@ -488,13 +506,13 @@
     copies = 2 + 3 * 28 + 2 * 28
     table = pltpu.VMEM((2, SIDE, SIDE * CAP, part), BF16)
     flops = 8 * 2 * rows * depth * width
-    anywhere, vmem = pl.BlockSpec(memory_space=pl.ANY), pl.BlockSpec(memory_space=pltpu.VMEM)
+    anywhere = pl.BlockSpec(memory_space=pl.ANY)
     block = jax.ShapeDtypeStruct((tokens, depth), BF16)
     routes = ids_a[0].T, gates_a[0].T, ids_b[0].T, gates_b[0].T
     x_here, grad, rows_a = pl.pallas_call(
         functools.partial(kernel, sections),
         out_shape=[block, block, jax.ShapeDtypeStruct((CAP, depth), BF16)],
-        in_specs=[vmem] * 5 + [anywhere] * 6,
+        in_specs=[anywhere] * 11,
         out_specs=[anywhere] * 3,
         scratch_shapes=[
             pltpu.VMEM((depth, width), BF16),
@@ -517,9 +535,15 @@
             pltpu.VMEM((2, 2, 2, CAP, part), BF16),
             pltpu.VMEM((tokens, CAP), BF16),
             pltpu.VMEM((2, CAP, depth), BF16),
+            pltpu.VMEM((2, tokens), jnp.int32),
+            pltpu.VMEM((2, tokens), F32),
+            pltpu.VMEM((2, tokens), jnp.int32),
+            pltpu.VMEM((2, tokens), F32),
+            pltpu.VMEM((1, depth), F32),
             pltpu.SemaphoreType.DMA((copies,)),
             pltpu.SemaphoreType.DMA((copies,)),
             pltpu.SemaphoreType.DMA((7,)),
+            pltpu.SemaphoreType.DMA((5,)),
         ],
         compiler_params=pltpu.CompilerParams(
             collective_id=0, has_side_effects=True, vmem_limit_bytes=60 * 1024 * 1024
@@ -531,13 +555,15 @@
     return pl.pallas_call(
         finish,
         out_shape=[jax.ShapeDtypeStruct(x_in.shape, BF16)] * 2,
-        in_specs=[vmem] * 2 + [anywhere] * 3,
+        in_specs=[anywhere] * 5,
         out_specs=[anywhere] * 2,
         scratch_shapes=[
+            pltpu.VMEM((2, tokens), jnp.int32),
+            pltpu.VMEM((2, tokens), F32),
             pltpu.VMEM((tokens, depth), BF16),
             pltpu.VMEM((tokens, depth), BF16),
             pltpu.VMEM((CAP, depth), BF16),
-            pltpu.SemaphoreType.DMA((17,)),
+            pltpu.SemaphoreType.DMA((19,)),
         ],
         compiler_params=pltpu.CompilerParams(vmem_limit_bytes=60 * 1024 * 1024),
     )(routes[0], routes[1], x_here, rows_a, grad)

time: 130 us -> 126 us (0.969)
  Pallas kernels: 129 us -> 125 us
    pallas_call x1, Pallas kernels: 125 us -> 123 us  [shards(): pl.pallas_call(functools.partial(kernel, sections), out_shape=[block, blo...]
where the time goes in v3:
time: 126 us
  Pallas kernels  125 us (99%)
    pallas_call x1, Pallas kernels, shards(): pl.pallas_call(functools.partial(kernel, sections), out_shape=[block, blo...  123 us
    pallas_call x1, Pallas kernels, shards(): pl.pallas_call(finish, out_shape=[jax.ShapeDtypeStruct(x_in.shape, BF16)]...  2.96 us

profile of v3, /device:TPU:0, one launch (start us, length us, event | category | flops | bytes accessed | tf_op | source)
XLA Modules:
  0.0 126.1 jit_solution(18153750049441422158)
XLA Ops:
  0.6 122.5 %shard_map.122 = (bf16[128,4096]{1,0:T(8,128)(2,1)}, bf16[128,4096]{1,0:T(8,128)(2,1)}, bf16[32,4096]{1,0:T(8,128)(2,1)}) custom-call(s32[2,128]{1,0:T(2,128)} %bitcast.12, f32[2,128]{1,0:T(2,128)} %bitcast.14, s32[2,128]{1,0:T(2,128)} %bitcast.16, f32[2,128]{1,0:T(2,128)} %bitcast.17, f32[1,4096]{1,0:T(1,128)} %gain_in.1, bf16[1,128,4096]{2,1,0:T(8,128)(2,1)} %x_in.1, ...), custom_call_target="tpu_custom_call" | custom-call | flops 25769803776 | bytes 24117248 | tf_op jit(solution)/shard_map/pallas_call | solution.py:512
  123.2 3.0 %shard_map.123 = (bf16[1,128,4096]{2,1,0:T(8,128)(2,1)}, bf16[1,128,4096]{2,1,0:T(8,128)(2,1)}) custom-call(s32[2,128]{1,0:T(2,128)} %bitcast.13, f32[2,128]{1,0:T(2,128)} %bitcast.15, bf16[128,4096]{1,0:T(8,128)(2,1)} %get-tuple-element.5.x_here, bf16[32,4096]{1,0:T(8,128)(2,1)} %get-tuple-element.6.rows_a, bf16[128,4096]{1,0:T(8,128)(2,1)} %get-tuple-element.7.grad), custom_call_target="tpu_custom_call" | custom-call | tf_op jit(solution)/shard_map/pallas_call | solution.py:555

commit v4 on v3

--- a/solution.py
+++ b/solution.py
@@ -278,6 +278,8 @@
                 + fin_f[t, h, MINUS].astype(F32)
             )
             rows_out[t, :, h * part : (h + 1) * part] = out.astype(BF16)
+            if t == 1:
+                write_rows[h].start()
 
     barrier = pltpu.get_barrier_semaphore()
     for device in (at_x(1), at_x(-1), at_z(1), at_z(-1), at_section(1), at_section(-1)):
@@ -288,15 +290,22 @@
             ((ids_b_in, ids_b), (gates_b_in, gates_b), (ids_a_in, ids_a), (gates_a_in, gates_a), (gain_in, gain_ref))
         )
     ]
-    load_saved = pltpu.make_async_copy(x_saved.at[0], saved, local_sem.at[0])
-    load_saved.start()
-    for copy in small:
+    quarter = tokens // 4
+    load_saved = [
+        pltpu.make_async_copy(x_saved.at[0, at], saved.at[at], local_sem.at[7 + k])
+        for k, at in enumerate(pl.ds(k * quarter, quarter) for k in range(4))
+    ]
+    for copy in load_saved + small:
         copy.start()
     loads = [
         pltpu.make_async_copy(src.at[0], dst, local_sem.at[k])
         for k, (src, dst) in enumerate(((w_gate, gate_w), (w_up, up_w), (w_down, down_w)), start=1)
     ]
     keep_x = pltpu.make_async_copy(x_here, x_out, local_sem.at[6])
+    write_rows = [
+        pltpu.make_async_copy(rows_out.at[1, :, at], rows_a_out.at[:, at], local_sem.at[k])
+        for k, at in ((0, pl.ds(0, part)), (5, pl.ds(part, part)))
+    ]
 
     for copy in small:
         copy.wait()
@@ -320,7 +329,8 @@
         scale = lax.rsqrt(jnp.mean(values * values, axis=-1, keepdims=True) + EPSILON)
         return (values * scale * gain_ref[...]).astype(BF16)
 
-    load_saved.wait()
+    for copy in load_saved:
+        copy.wait()
     put_own(tab_b, normed(dot(take_b, saved[...])))
     def rows_c():
         copy_dy.wait_recv()
@@ -445,15 +455,12 @@
         grad = cot[at, :].astype(F32) + scale * (weighted - values * scale * scale * average)
         cot[at, :] = grad.astype(BF16)
 
-    pl.loop(0, 2)(grad_part)
     scatter_3(scatter_a, tab_c, 1)
-    pl.loop(2, 4)(grad_part)
+    pl.loop(0, 4)(grad_part)
     write_grad = pltpu.make_async_copy(cot, grad_out, local_sem.at[4])
     write_grad.start()
     scatter_own(scatter_a, tab_c, 1)
     scatter_4(scatter_a, tab_c, 1)
-    write_rows = pltpu.make_async_copy(rows_out.at[1], rows_a_out, local_sem.at[5])
-    write_rows.start()
     sent(gather_a)
     sent(scatter_b)
     sent(scatter_a)
@@ -461,7 +468,8 @@
     copy_dy.wait_send()
     keep_x.wait()
     write_grad.wait()
-    write_rows.wait()
+    for copy in write_rows:
+        copy.wait()
 
 
 def finish(ids_in, gates_in, x_here, rows_a, grad, mixed_out, grad_out, ids_a, gates_a, x_part, grad_part, rows, sem):
@@ -542,7 +550,7 @@
             pltpu.VMEM((1, depth), F32),
             pltpu.SemaphoreType.DMA((copies,)),
             pltpu.SemaphoreType.DMA((copies,)),
-            pltpu.SemaphoreType.DMA((7,)),
+            pltpu.SemaphoreType.DMA((11,)),
             pltpu.SemaphoreType.DMA((5,)),
         ],
         compiler_params=pltpu.CompilerParams(

time: 126 us -> 126 us (level)
  no operation moved by 1% of the time
where the time goes in v4:
time: 126 us
  Pallas kernels  125 us (99%)
    pallas_call x1, Pallas kernels, shards(): pl.pallas_call(functools.partial(kernel, sections), out_shape=[block, blo...  122 us
    pallas_call x1, Pallas kernels, shards(): pl.pallas_call(finish, out_shape=[jax.ShapeDtypeStruct(x_in.shape, BF16)]...  2.97 us

profile of v4, /device:TPU:0, one launch (start us, length us, event | category | flops | bytes accessed | tf_op | source)
XLA Modules:
  0.0 125.6 jit_solution(4463648701714124786)
XLA Ops:
  0.6 122.0 %shard_map.122 = (bf16[128,4096]{1,0:T(8,128)(2,1)}, bf16[128,4096]{1,0:T(8,128)(2,1)}, bf16[32,4096]{1,0:T(8,128)(2,1)}) custom-call(s32[2,128]{1,0:T(2,128)} %bitcast.12, f32[2,128]{1,0:T(2,128)} %bitcast.14, s32[2,128]{1,0:T(2,128)} %bitcast.16, f32[2,128]{1,0:T(2,128)} %bitcast.17, f32[1,4096]{1,0:T(1,128)} %gain_in.1, bf16[1,128,4096]{2,1,0:T(8,128)(2,1)} %x_in.1, ...), custom_call_target="tpu_custom_call" | custom-call | flops 25769803776 | bytes 24117248 | tf_op jit(solution)/shard_map/pallas_call | solution.py:520
  122.7 3.0 %shard_map.123 = (bf16[1,128,4096]{2,1,0:T(8,128)(2,1)}, bf16[1,128,4096]{2,1,0:T(8,128)(2,1)}) custom-call(s32[2,128]{1,0:T(2,128)} %bitcast.13, f32[2,128]{1,0:T(2,128)} %bitcast.15, bf16[128,4096]{1,0:T(8,128)(2,1)} %get-tuple-element.5.x_here, bf16[32,4096]{1,0:T(8,128)(2,1)} %get-tuple-element.6.rows_a, bf16[128,4096]{1,0:T(8,128)(2,1)} %get-tuple-element.7.grad), custom_call_target="tpu_custom_call" | custom-call | tf_op jit(solution)/shard_map/pallas_call | solution.py:563

commit v5 on v4

--- a/solution.py
+++ b/solution.py
@@ -474,18 +474,22 @@
 
 def finish(ids_in, gates_in, x_here, rows_a, grad, mixed_out, grad_out, ids_a, gates_a, x_part, grad_part, rows, sem):
     tokens = x_part.shape[0]
-    chunk = tokens // 4
-    load_rows = pltpu.make_async_copy(rows_a, rows, sem.at[8])
-    load_ids = pltpu.make_async_copy(ids_in, ids_a, sem.at[17])
-    load_gates = pltpu.make_async_copy(gates_in, gates_a, sem.at[18])
-    for copy in (load_ids, load_gates, load_rows):
+    pieces = 8
+    chunk = tokens // pieces
+    load_ids = pltpu.make_async_copy(ids_in, ids_a, sem.at[40])
+    load_gates = pltpu.make_async_copy(gates_in, gates_a, sem.at[41])
+    for copy in (load_ids, load_gates):
         copy.start()
-    chunks = [pl.ds(i * chunk, chunk) for i in range(4)]
-    wide = x_part.shape[1] // 4
-    strips = [pl.ds(i * wide, wide) for i in range(4)]
+    chunks = [pl.ds(i * chunk, chunk) for i in range(pieces)]
+    wide = x_part.shape[1] // pieces
+    strips = [pl.ds(i * wide, wide) for i in range(pieces)]
+    load_rows = [pltpu.make_async_copy(rows_a.at[:, at], rows.at[:, at], sem.at[16 + i]) for i, at in enumerate(strips)]
     loads = [pltpu.make_async_copy(x_here.at[:, at], x_part.at[:, at], sem.at[i]) for i, at in enumerate(strips)]
-    takes = [pltpu.make_async_copy(grad.at[at], grad_part.at[at], sem.at[4 + i]) for i, at in enumerate(chunks)]
-    for copy in loads + takes:
+    takes = [pltpu.make_async_copy(grad.at[at], grad_part.at[at], sem.at[8 + i]) for i, at in enumerate(chunks)]
+    for i in range(pieces):
+        load_rows[i].start()
+        loads[i].start()
+    for copy in takes:
         copy.start()
     load_ids.wait()
     load_gates.wait()
@@ -493,15 +497,15 @@
     place = (column(slot_code(flag)) == lax.broadcasted_iota(jnp.int32, (tokens, CAP), 1).astype(F32)).astype(F32)
     place = place.astype(BF16)
     share = column(share)
-    load_rows.wait()
     writes = []
     for i, (at, strip) in enumerate(zip(chunks, strips)):
+        load_rows[i].wait()
         loads[i].wait()
         x_part[:, strip] = (x_part[:, strip].astype(F32) + share * dot(place, rows[:, strip])).astype(BF16)
-        writes.append(pltpu.make_async_copy(x_part.at[:, strip], mixed_out.at[0, :, strip], sem.at[9 + i]))
+        writes.append(pltpu.make_async_copy(x_part.at[:, strip], mixed_out.at[0, :, strip], sem.at[24 + i]))
         writes[-1].start()
         takes[i].wait()
-        writes.append(pltpu.make_async_copy(grad_part.at[at], grad_out.at[0, at], sem.at[13 + i]))
+        writes.append(pltpu.make_async_copy(grad_part.at[at], grad_out.at[0, at], sem.at[32 + i]))
         writes[-1].start()
     for write in writes:
         write.wait()
@@ -571,7 +575,7 @@
             pltpu.VMEM((tokens, depth), BF16),
             pltpu.VMEM((tokens, depth), BF16),
             pltpu.VMEM((CAP, depth), BF16),
-            pltpu.SemaphoreType.DMA((19,)),
+            pltpu.SemaphoreType.DMA((42,)),
         ],
         compiler_params=pltpu.CompilerParams(vmem_limit_bytes=60 * 1024 * 1024),
     )(routes[0], routes[1], x_here, rows_a, grad)

time: 126 us -> 127 us (level)
  no operation moved by 1% of the time
where the time goes in v5:
time: 127 us; the launch traced here: 126 us
  Pallas kernels  126 us (99%)
    pallas_call x1, Pallas kernels, shards(): pl.pallas_call(functools.partial(kernel, sections), out_shape=[block, blo...  122 us
    pallas_call x1, Pallas kernels, shards(): pl.pallas_call(finish, out_shape=[jax.ShapeDtypeStruct(x_in.shape, BF16)]...  3.69 us

profile of v5, /device:TPU:0, one launch (start us, length us, event | category | flops | bytes accessed | tf_op | source)
XLA Modules:
  0.0 126.4 jit_solution(6874177912274992331)
XLA Ops:
  0.6 122.0 %shard_map.122 = (bf16[128,4096]{1,0:T(8,128)(2,1)}, bf16[128,4096]{1,0:T(8,128)(2,1)}, bf16[32,4096]{1,0:T(8,128)(2,1)}) custom-call(s32[2,128]{1,0:T(2,128)} %bitcast.12, f32[2,128]{1,0:T(2,128)} %bitcast.14, s32[2,128]{1,0:T(2,128)} %bitcast.16, f32[2,128]{1,0:T(2,128)} %bitcast.17, f32[1,4096]{1,0:T(1,128)} %gain_in.1, bf16[1,128,4096]{2,1,0:T(8,128)(2,1)} %x_in.1, ...), custom_call_target="tpu_custom_call" | custom-call | flops 25769803776 | bytes 24117248 | tf_op jit(solution)/shard_map/pallas_call | solution.py:524
  122.7 3.7 %shard_map.123 = (bf16[1,128,4096]{2,1,0:T(8,128)(2,1)}, bf16[1,128,4096]{2,1,0:T(8,128)(2,1)}) custom-call(s32[2,128]{1,0:T(2,128)} %bitcast.13, f32[2,128]{1,0:T(2,128)} %bitcast.15, bf16[128,4096]{1,0:T(8,128)(2,1)} %get-tuple-element.5.x_here, bf16[32,4096]{1,0:T(8,128)(2,1)} %get-tuple-element.6.rows_a, bf16[128,4096]{1,0:T(8,128)(2,1)} %get-tuple-element.7.grad), custom_call_target="tpu_custom_call" | custom-call | tf_op jit(solution)/shard_map/pallas_call | solution.py:567
